TPU v7x, 32 devices: a whole 2x2x4 slice. The times are simulated.
32 devices in a mesh: dom: 16 (over z, y, core), mode: 2 (over x).
Axes of the slice: x: 2, y: 2, z: 4, core: 2. Of those that a mesh axis runs over, the one named last changes fastest.
Arguments:
- mode_basis: bfloat16 [3, 512, 16384], P(None, 'mode', 'dom'), may hold values from -6 to 6
- blocks: bfloat16 [16, 3, 3, 16384], P(None, None, None, 'dom'), may hold values from -0.875 to 0.875
- columns: int32 [16, 16384], P(None, 'dom'), may hold values from -256 to 257, as said below
- samples: int32 [512], replicated, may hold values from 0 to 49151, as said below
- inverse: bfloat16 [512, 512], replicated, may hold values from -0.25 to 0.25
Outputs:
- reduced: float32 [512, 512], P('dom', 'mode')
- coefficients: float32 [512, 512], P('dom', 'mode')
Inputs may be any that keep to these rules, and one draw needn't show every extreme that they name: `columns`: each entry is 256 + 1 (an empty slot) or an offset that keeps n + offset within 0 to 16383; slot 0 of every row holds offset 0. `samples`: 512 distinct dofs; half of them lie in the first half of the dofs.
All inputs are finite; a program needn't handle non-finite values.
Results may differ from a plain program's by a relative error of at most 0.0029.
Values may be sent and summed in bfloat16 or wider, within the bound.
A program may use at most 64 MiB of HBM per device.

v0:
```python
import math

import jax
import jax.numpy as jnp
from jax import lax
from jax.sharding import PartitionSpec as P


def extended_2(x, sides, width):
    for axis, dim in sides:
        devices, length = (lax.axis_size(axis), x.shape[dim])
        up = [(i, (i + 1) % devices) for i in range(devices - 1)]
        down = [(j, i) for i, j in up]
        last = lax.slice_in_dim(x, length - width, length, axis=dim)
        initial = lax.slice_in_dim(x, 0, width, axis=dim)
        before = lax.ppermute(last, axis, up)
        after = lax.ppermute(initial, axis, down)
        x = jnp.concatenate([before, x, after], axis=dim)
    return x


def slot_products(extended, blocks, columns, halo_width, out_shape):
    local_ids = lax.broadcasted_iota(jnp.int32, (out_shape[2],), 0)

    def slot_step(slot_index, running):
        offset = columns[slot_index]
        usable = offset != halo_width + 1
        position = jnp.where(usable, local_ids + offset + halo_width, 0)
        nearby = jnp.take(extended, position, axis=2)
        weights = jnp.where(
            usable[None, None, :], blocks[slot_index].astype(jnp.float32), jnp.float32(0.0)
        )
        running = running + weights[:, 0, None, :] * nearby[0][None]
        running = running + weights[:, 1, None, :] * nearby[1][None]
        running = running + weights[:, 2, None, :] * nearby[2][None]
        return running

    return lax.fori_loop(0, blocks.shape[0], slot_step, jnp.zeros(out_shape, jnp.float32))


def shards(mode_basis, blocks, columns, samples, inverse):
    node_count = mode_basis.shape[2]
    halo_width = node_count // 4
    first_node = lax.axis_index("dom") * node_count
    extended = extended_2(mode_basis, (("dom", 2),), halo_width)
    image = slot_products(extended, blocks, columns, halo_width, mode_basis.shape).astype(
        jnp.bfloat16
    )
    scaling = 1.0 / math.sqrt(3 * node_count * lax.axis_size("dom"))
    reduced_part = jnp.einsum(
        "crn,csn->rs",
        lax.all_gather(mode_basis, "mode", axis=1, tiled=True),
        image,
        preferred_element_type=jnp.float32,
    )
    component = samples % 3
    node_index = samples // 3 - first_node
    owned_here = (node_index >= 0) & (node_index < node_count)
    node_local = jnp.where(owned_here, node_index, 0)
    chosen = image[component, :, node_local]
    chosen = jnp.where(owned_here[:, None], chosen, jnp.zeros_like(chosen))
    reduced = lax.psum_scatter(reduced_part, "dom", scatter_dimension=0, tiled=True)
    picked = lax.psum(chosen.astype(jnp.float32), "dom").astype(jnp.bfloat16)
    row_count = inverse.shape[0] // lax.axis_size("dom")
    inverse_rows = lax.dynamic_slice_in_dim(
        inverse, lax.axis_index("dom") * row_count, row_count, 0
    )
    coefficients = jnp.dot(inverse_rows, picked, preferred_element_type=jnp.float32)
    return (reduced * scaling, coefficients)


def solution(mesh):
    return jax.shard_map(
        shards,
        mesh=mesh,
        in_specs=(P(None, "mode", "dom"), P(None, None, None, "dom"), P(None, "dom"), P(), P()),
        out_specs=(P("dom", "mode"), P("dom", "mode")),
        check_vma=False,
    )
```

profile of v0, /device:TPU:0, one launch (start us, length us, event | category | flops | bytes accessed | tf_op | source)
XLA Modules:
  0.0 531.8 jit_solution(7872869750765811868)
XLA Ops:
  20.3 8.8 %pad_maximum_fusion = bf16[3,256,1536]{1,0,2:T(4,128)(2,1)} fusion(bf16[3,256,256]{1,0,2:T(4,128)(2,1)} %collective-permute-done.1, bf16[3,256,1024]{1,0,2:T(4,128)(2,1)S(1)} %copy.24, bf16[3,256,256]{1,0,2:T(4,128)(2,1)} %collective-permute-done), kind=kLoop, calls=%fused_computation.26 | loop fusion | flops 2359296 | bytes 4718592 | tf_op jit(solution)/shard_map/concatenate | solution.py:18
  29.0 411.3 %while.15 = (s32[]{:T(128)}, f32[3,256,1024]{2,1,0:T(8,128)}, s32[16,1024]{1,0:T(8,128)}, bf16[16,3,3,1024]{3,1,2,0:T(4,128)(2,1)S(1)}, bf16[3,256,1536]{1,0,2:T(4,128)(2,1)}, /*index=5*/s32[]{:T(128)}, s32[]{:T(128)}) while((s32[]{:T(128)}, f32[3,256,1024]{2,1,0:T(8,128)}, s32[16,1024]{1,0:T(8,128)}, ...), condition=%wide.region_1.2_spmd.clone.clone, body=%wide.region_0.1_spmd.clone.clone.sunk | while | flops 7114755 | bytes 26937436 | solution.py:38
  29.8 6.1 %gather_fusion = bf16[1024,3,256]{2,1,0:T(4,128)(2,1)S(1)} fusion(bf16[3,256,1536]{1,0,2:T(4,128)(2,1)} %get-tuple-element.265, s32[1024]{0:T(1024)S(1)} %broadcast_clamp_fusion.2), kind=kCustom, calls=%fused_computation.clone.clone.1 | custom fusion | bytes 3149824 | tf_op jit(solution)/shard_map/while/body/eval_jaxpr/jit(_take)/gather | solution.py:29
  54.9 5.8 %gather_fusion = bf16[1024,3,256]{2,1,0:T(4,128)(2,1)S(1)} fusion(bf16[3,256,1536]{1,0,2:T(4,128)(2,1)} %get-tuple-element.265, s32[1024]{0:T(1024)S(1)} %broadcast_clamp_fusion.2), kind=kCustom, calls=%fused_computation.clone.clone.1 | custom fusion | bytes 3149824 | tf_op jit(solution)/shard_map/while/body/eval_jaxpr/jit(_take)/gather | solution.py:29
  75.1 4.8 fusion.23
  80.7 5.8 %gather_fusion = bf16[1024,3,256]{2,1,0:T(4,128)(2,1)S(1)} fusion(bf16[3,256,1536]{1,0,2:T(4,128)(2,1)} %get-tuple-element.265, s32[1024]{0:T(1024)S(1)} %broadcast_clamp_fusion.2), kind=kCustom, calls=%fused_computation.clone.clone.1 | custom fusion | bytes 3149824 | tf_op jit(solution)/shard_map/while/body/eval_jaxpr/jit(_take)/gather | solution.py:29
  100.8 4.8 fusion.23
  106.4 5.8 %gather_fusion = bf16[1024,3,256]{2,1,0:T(4,128)(2,1)S(1)} fusion(bf16[3,256,1536]{1,0,2:T(4,128)(2,1)} %get-tuple-element.265, s32[1024]{0:T(1024)S(1)} %broadcast_clamp_fusion.2), kind=kCustom, calls=%fused_computation.clone.clone.1 | custom fusion | bytes 3149824 | tf_op jit(solution)/shard_map/while/body/eval_jaxpr/jit(_take)/gather | solution.py:29
  126.6 4.8 fusion.23
  132.2 5.8 %gather_fusion = bf16[1024,3,256]{2,1,0:T(4,128)(2,1)S(1)} fusion(bf16[3,256,1536]{1,0,2:T(4,128)(2,1)} %get-tuple-element.265, s32[1024]{0:T(1024)S(1)} %broadcast_clamp_fusion.2), kind=kCustom, calls=%fused_computation.clone.clone.1 | custom fusion | bytes 3149824 | tf_op jit(solution)/shard_map/while/body/eval_jaxpr/jit(_take)/gather | solution.py:29
  152.3 4.8 fusion.23
  157.9 5.8 %gather_fusion = bf16[1024,3,256]{2,1,0:T(4,128)(2,1)S(1)} fusion(bf16[3,256,1536]{1,0,2:T(4,128)(2,1)} %get-tuple-element.265, s32[1024]{0:T(1024)S(1)} %broadcast_clamp_fusion.2), kind=kCustom, calls=%fused_computation.clone.clone.1 | custom fusion | bytes 3149824 | tf_op jit(solution)/shard_map/while/body/eval_jaxpr/jit(_take)/gather | solution.py:29
  178.1 4.8 fusion.23
  183.7 5.8 %gather_fusion = bf16[1024,3,256]{2,1,0:T(4,128)(2,1)S(1)} fusion(bf16[3,256,1536]{1,0,2:T(4,128)(2,1)} %get-tuple-element.265, s32[1024]{0:T(1024)S(1)} %broadcast_clamp_fusion.2), kind=kCustom, calls=%fused_computation.clone.clone.1 | custom fusion | bytes 3149824 | tf_op jit(solution)/shard_map/while/body/eval_jaxpr/jit(_take)/gather | solution.py:29
  209.4 5.8 %gather_fusion = bf16[1024,3,256]{2,1,0:T(4,128)(2,1)S(1)} fusion(bf16[3,256,1536]{1,0,2:T(4,128)(2,1)} %get-tuple-element.265, s32[1024]{0:T(1024)S(1)} %broadcast_clamp_fusion.2), kind=kCustom, calls=%fused_computation.clone.clone.1 | custom fusion | bytes 3149824 | tf_op jit(solution)/shard_map/while/body/eval_jaxpr/jit(_take)/gather | solution.py:29
  235.2 5.8 %gather_fusion = bf16[1024,3,256]{2,1,0:T(4,128)(2,1)S(1)} fusion(bf16[3,256,1536]{1,0,2:T(4,128)(2,1)} %get-tuple-element.265, s32[1024]{0:T(1024)S(1)} %broadcast_clamp_fusion.2), kind=kCustom, calls=%fused_computation.clone.clone.1 | custom fusion | bytes 3149824 | tf_op jit(solution)/shard_map/while/body/eval_jaxpr/jit(_take)/gather | solution.py:29
  260.9 5.8 %gather_fusion = bf16[1024,3,256]{2,1,0:T(4,128)(2,1)S(1)} fusion(bf16[3,256,1536]{1,0,2:T(4,128)(2,1)} %get-tuple-element.265, s32[1024]{0:T(1024)S(1)} %broadcast_clamp_fusion.2), kind=kCustom, calls=%fused_computation.clone.clone.1 | custom fusion | bytes 3149824 | tf_op jit(solution)/shard_map/while/body/eval_jaxpr/jit(_take)/gather | solution.py:29
  286.7 5.8 %gather_fusion = bf16[1024,3,256]{2,1,0:T(4,128)(2,1)S(1)} fusion(bf16[3,256,1536]{1,0,2:T(4,128)(2,1)} %get-tuple-element.265, s32[1024]{0:T(1024)S(1)} %broadcast_clamp_fusion.2), kind=kCustom, calls=%fused_computation.clone.clone.1 | custom fusion | bytes 3149824 | tf_op jit(solution)/shard_map/while/body/eval_jaxpr/jit(_take)/gather | solution.py:29
  312.4 5.8 %gather_fusion = bf16[1024,3,256]{2,1,0:T(4,128)(2,1)S(1)} fusion(bf16[3,256,1536]{1,0,2:T(4,128)(2,1)} %get-tuple-element.265, s32[1024]{0:T(1024)S(1)} %broadcast_clamp_fusion.2), kind=kCustom, calls=%fused_computation.clone.clone.1 | custom fusion | bytes 3149824 | tf_op jit(solution)/shard_map/while/body/eval_jaxpr/jit(_take)/gather | solution.py:29
  338.2 5.8 %gather_fusion = bf16[1024,3,256]{2,1,0:T(4,128)(2,1)S(1)} fusion(bf16[3,256,1536]{1,0,2:T(4,128)(2,1)} %get-tuple-element.265, s32[1024]{0:T(1024)S(1)} %broadcast_clamp_fusion.2), kind=kCustom, calls=%fused_computation.clone.clone.1 | custom fusion | bytes 3149824 | tf_op jit(solution)/shard_map/while/body/eval_jaxpr/jit(_take)/gather | solution.py:29
  363.9 5.8 %gather_fusion = bf16[1024,3,256]{2,1,0:T(4,128)(2,1)S(1)} fusion(bf16[3,256,1536]{1,0,2:T(4,128)(2,1)} %get-tuple-element.265, s32[1024]{0:T(1024)S(1)} %broadcast_clamp_fusion.2), kind=kCustom, calls=%fused_computation.clone.clone.1 | custom fusion | bytes 3149824 | tf_op jit(solution)/shard_map/while/body/eval_jaxpr/jit(_take)/gather | solution.py:29
  389.6 5.8 %gather_fusion = bf16[1024,3,256]{2,1,0:T(4,128)(2,1)S(1)} fusion(bf16[3,256,1536]{1,0,2:T(4,128)(2,1)} %get-tuple-element.265, s32[1024]{0:T(1024)S(1)} %broadcast_clamp_fusion.2), kind=kCustom, calls=%fused_computation.clone.clone.1 | custom fusion | bytes 3149824 | tf_op jit(solution)/shard_map/while/body/eval_jaxpr/jit(_take)/gather | solution.py:29
  415.4 5.8 %gather_fusion = bf16[1024,3,256]{2,1,0:T(4,128)(2,1)S(1)} fusion(bf16[3,256,1536]{1,0,2:T(4,128)(2,1)} %get-tuple-element.265, s32[1024]{0:T(1024)S(1)} %broadcast_clamp_fusion.2), kind=kCustom, calls=%fused_computation.clone.clone.1 | custom fusion | bytes 3149824 | tf_op jit(solution)/shard_map/while/body/eval_jaxpr/jit(_take)/gather | solution.py:29
  449.9 72.7 %all-reduce.1 = bf16[512,256]{1,0:T(8,128)(2,1)S(1)} all-reduce(f32[512,256]{1,0:T(8,128)S(1)} %select_convert_fusion), channel_id=1, replica_groups=mesh['dom'=16,'mode'=2] {'dom'}, use_global_device_ids=true, to_apply=%region_3.4 | all-reduce | flops 131072 | bytes 786432 | tf_op jit(solution)/shard_map/psum | solution.py:63
  (201 shorter events, 317.6 us)
Async XLA Ops:
  7.2 515.5 %copy-start = (bf16[512,512]{1,0:T(8,128)(2,1)S(1)}, bf16[512,512]{1,0:T(8,128)(2,1)}, u32[]{:S(2)}) copy-start(bf16[512,512]{1,0:T(8,128)(2,1)} %param.11) | copy-start | bytes 1572868
  7.2 9.0 %copy-start.1 = (bf16[16,3,3,1024]{3,0,2,1:T(8,128)(2,1)S(1)}, bf16[16,3,3,1024]{3,0,2,1:T(8,128)(2,1)}, u32[]{:S(2)}) copy-start(bf16[16,3,3,1024]{3,0,2,1:T(8,128)(2,1)} %param.8) | copy-start | bytes 884740
  7.2 435.3 %all-gather.2.cloned.1.call-start = ((), (), s32[]{:S(2)}) async-start(), calls=%async_computation.1 | async-start | bytes 4718592 | tf_op jit(solution)/shard_map/all_gather | solution.py:52
  11.6 4.8 collective-permute-start
  14.8 5.5 %collective-permute-start.1 = (bf16[3,256,256]{1,0,2:T(4,128)(2,1)}, bf16[3,256,256]{1,0,2:T(4,128)(2,1)}, u32[]{:S(2)}, u32[]{:S(2)}) collective-permute-start(bf16[3,256,256]{1,0,2:T(4,128)(2,1)} %get-tuple-element.195), channel_id=1, source_target_pairs={{2,0},{4,2},{6,4},{8,6},{10,8},{12,10},{14,12},{16,14},{18,16},{20... | collective-permute-start | bytes 1179656 | tf_op jit(solution)/shard_map/ppermute | solution.py:17
  16.1 507.3 %reduce-scatter.4.cloned.1.call-start = ((), (), s32[]{:S(2)}) async-start(), calls=%async_computation.2 | async-start | bytes 557056
  442.5 4.0 copy-start.2
Sparse Core Ops, SparseCore 0:
  16.2 48.7 all-gather.1
  446.6 65.7 reduce-scatter.3
where the time goes:
time: 536 us; the launch traced here: 532 us
  local copies, waits for them, and re-layouts  223 us (42%)
  other arithmetic  209 us (39%)
  blocking collectives  72.7 us (14%)
  between operations  14.2 us (3%)
    gather x16, local copies, waits for them, and re-layouts, slot_step(): nearby = jnp.take(extended, position, axis=2)  93.5 us
    add x16, other arithmetic, slot_step(): running = running + weights[:, 2, None, :] * nearby[2][None]  75.5 us
    select_n x32, other arithmetic, slot_step(): nearby = jnp.take(extended, position, axis=2)  73.5 us
    psum x1, blocking collectives, shards(): picked = lax.psum(chosen.astype(jnp.float32), 'dom').astype(jnp.bfloat16)  72.7 us
    mul x32, local copies, waits for them, and re-layouts, slot_step(): running = running + weights[:, 0, None, :] * nearby[0][None]  57.9 us
    mul x16, other arithmetic, slot_step(): running = running + weights[:, 0, None, :] * nearby[0][None]  50.6 us
    mul x16, local copies, waits for them, and re-layouts, slot_step(): running = running + weights[:, 1, None, :] * nearby[1][None]  37.7 us
    mul x16, local copies, waits for them, and re-layouts, slot_step(): running = running + weights[:, 2, None, :] * nearby[2][None]  20.9 us
  transfers between devices with their start and end apart: 4, of which 1 were waited for; matrix products, arithmetic and copies ran while one was open for 80% of the time, Pallas kernels for 0%

commit v1 on v0

v1 whole, which is shorter than its diff:
```python
import functools
import math

import jax
import jax.numpy as jnp
from jax import lax
from jax.experimental import pallas as pl
from jax.experimental.pallas import tpu as pltpu
from jax.sharding import PartitionSpec as P

MESH = pl.DeviceIdType.MESH
LANES = 128
ROWS = 64
F32, BF16 = jnp.float32, jnp.bfloat16


def dot_nt(a, b):
    return lax.dot_general(a, b, (((1,), (1,)), ((), ())), preferred_element_type=F32)


def kernel(
    doms, modes, halo, scaling,
    basis, blocks, columns, samples, inverse,
    reduced_out, coef_out,
    ext, other, image, weights, spread, onehot, chosen, coef, part, coef_in, part_in,
    local_sem, halo_send, halo_recv, gather_send, gather_recv,
    coef_send, coef_recv, part_send, part_recv,
):
    slots = columns.shape[0]
    modes_here, nodes = basis.shape[1], basis.shape[2]
    rows = reduced_out.shape[0]
    group = doms // modes
    window = LANES + 2 * halo
    tiles = nodes // LANES
    dom, mode = lax.axis_index("dom"), lax.axis_index("mode")

    def at_dom(target):
        return (target, mode)

    barrier = pltpu.get_barrier_semaphore()

    def greet(step, carry):
        pl.semaphore_signal(barrier, inc=1, device_id=at_dom(lax.rem(dom + step, doms)), device_id_type=MESH)
        return carry

    lax.fori_loop(1, doms, greet, 0)
    for step in range(1, modes):
        pl.semaphore_signal(barrier, inc=1, device_id=(dom, lax.rem(mode + step, modes)), device_id_type=MESH)

    local = pltpu.make_async_copy(basis, ext.at[:, :, pl.ds(halo, nodes)], local_sem)
    local.start()
    pl.semaphore_wait(barrier, doms + modes - 2)

    up = pltpu.make_async_remote_copy(
        basis.at[:, :, pl.ds(nodes - halo, halo)], ext.at[:, :, pl.ds(0, halo)],
        halo_send.at[0], halo_recv.at[0], at_dom(lax.rem(dom + 1, doms)), MESH,
    )
    down = pltpu.make_async_remote_copy(
        basis.at[:, :, pl.ds(0, halo)], ext.at[:, :, pl.ds(halo + nodes, halo)],
        halo_send.at[1], halo_recv.at[1], at_dom(lax.rem(dom + doms - 1, doms)), MESH,
    )

    @pl.when(dom < doms - 1)
    def _():
        up.start()

    @pl.when(dom > 0)
    def _():
        down.start()

    gathers = []
    for c in range(3):
        for step in range(1, modes):
            copy = pltpu.make_async_remote_copy(
                basis.at[c], other.at[step - 1, c],
                gather_send.at[step - 1, c], gather_recv.at[step - 1, c],
                (dom, lax.rem(mode + step, modes)), MESH,
            )
            copy.start()
            gathers.append(copy)

    @pl.when(dom == 0)
    def _():
        ext[:, :, pl.ds(0, halo)] = jnp.zeros((3, modes_here, halo), BF16)

    @pl.when(dom == doms - 1)
    def _():
        ext[:, :, pl.ds(halo + nodes, halo)] = jnp.zeros((3, modes_here, halo), BF16)

    row_ids = (
        lax.broadcasted_iota(jnp.int32, (ROWS // 16, 16, LANES), 0) * 16
        + lax.broadcasted_iota(jnp.int32, (ROWS // 16, 16, LANES), 1)
    ).astype(F32).astype(BF16)
    lane_ids = lax.broadcasted_iota(jnp.int32, (1, LANES), 1)

    def tile_step(step, carry):
        tile = lax.rem(step + tiles // 4, tiles)
        start = pl.multiple_of(tile * LANES, LANES)
        here = pl.ds(start, LANES)

        offsets, values = [], []
        for j in range(slots):
            offset = columns[pl.ds(j, 1), here]
            offsets.append(jnp.where(offset == halo + 1, -8 * halo - j, offset))
            values.append([blocks[j, a, :, here].astype(F32) for a in range(3)])
        for i in range(slots):
            for j in range(i + 1, slots):
                same = offsets[j] == offsets[i]
                for a in range(3):
                    values[i][a] = values[i][a] + jnp.where(same, values[j][a], 0.0)
                offsets[j] = jnp.where(same, -8 * halo - j, offsets[j])
        for j in range(slots):
            for a in range(3):
                for b in range(3):
                    spread[j, 3 * a + b] = jnp.broadcast_to(
                        values[j][a][b:b + 1], (16, LANES)
                    ).astype(BF16)
        places = [(offset + lane_ids + halo).astype(F32) for offset in offsets]

        def row_step(segment, inner):
            base = (segment * ROWS).astype(F32)
            sums = [jnp.zeros((ROWS // 16, 16, LANES), BF16) for _ in range(9)]
            for j in range(slots):
                place = jnp.broadcast_to(places[j] - base, (16, LANES)).astype(BF16)
                hit = row_ids == place[None]
                for k in range(9):
                    sums[k] = jnp.where(hit, spread[j, k][None], sums[k])
            span = pl.ds(pl.multiple_of(segment * ROWS, ROWS), ROWS)
            for a in range(3):
                for b in range(3):
                    weights[b, span, a * LANES:(a + 1) * LANES] = sums[3 * a + b].reshape(ROWS, LANES)
            return inner

        lax.fori_loop(0, window // ROWS, row_step, 0)

        @pl.when(step == 0)
        def _():
            local.wait()

        @pl.when(step == tiles // 2)
        def _():
            @pl.when(dom > 0)
            def _():
                up.wait_recv()

            @pl.when(dom < doms - 1)
            def _():
                down.wait_recv()

        total = jnp.zeros((modes_here, 3 * LANES), F32)
        for b in range(3):
            total = total + jnp.dot(
                ext[b, :, pl.ds(start, window)], weights[b], preferred_element_type=F32
            )
        for a in range(3):
            image[a, :, here] = total[:, a * LANES:(a + 1) * LANES].astype(BF16)
        return carry

    lax.fori_loop(0, tiles, tile_step, 0)

    dofs = samples[...] - 3 * nodes * dom
    sample_count = dofs.shape[1]
    chosen[...] = jnp.zeros_like(chosen)
    node_ids = 3 * lax.broadcasted_iota(jnp.int32, (LANES, sample_count), 0)
    for c in range(3):
        def mark(tile, carry):
            found = node_ids == dofs - (3 * LANES * tile + c)
            onehot[pl.ds(pl.multiple_of(tile * LANES, LANES), LANES), :] = jnp.where(found, 1.0, 0.0).astype(BF16)
            return carry

        lax.fori_loop(0, tiles, mark, 0)
        chosen[...] += jnp.dot(image[c], onehot[...], preferred_element_type=F32)
    coef[...] = dot_nt(inverse[...], chosen[...].astype(BF16))

    def rows_of(target):
        return pl.ds(pl.multiple_of(target * rows, 8), rows)

    def slot_at(target):
        return lax.rem(dom - target + doms, doms) - 1

    def coef_copy(step):
        target = lax.rem(dom + step, doms)
        slot = doms - step - 1
        return pltpu.make_async_remote_copy(
            coef.at[rows_of(target)], coef_in.at[slot], coef_send.at[step - 1], coef_recv.at[slot],
            at_dom(target), MESH,
        )

    def send_coef(step, carry):
        coef_copy(step).start()
        return carry

    lax.fori_loop(1, doms, send_coef, 0)

    def part_copy(target):
        slot = lax.rem(dom - target + doms - 1 + doms, doms)
        return pltpu.make_async_remote_copy(
            part.at[rows_of(target)], part_in.at[slot], part_send.at[target], part_recv.at[slot],
            at_dom(target), MESH,
        )

    def send_parts(block):
        def send(g, carry):
            target = block * group + g

            @pl.when(target != dom)
            def _():
                part_copy(target).start()

            return carry

        lax.fori_loop(0, group, send, 0)

    def block_rows(block):
        return pl.ds(pl.multiple_of(block * modes_here, 8), modes_here)

    total = jnp.zeros((modes_here, modes_here), F32)
    for c in range(3):
        total = total + dot_nt(ext[c, :, pl.ds(halo, nodes)], image[c])
    part[block_rows(mode)] = total
    send_parts(mode)

    for step in range(1, modes):
        block = lax.rem(mode + modes - step, modes)
        total = jnp.zeros((modes_here, modes_here), F32)
        for c in range(3):
            gathers[c * (modes - 1) + step - 1].wait_recv()
            total = total + dot_nt(other[step - 1, c], image[c])
        part[block_rows(block)] = total
        send_parts(block)

    coef_out[...] = coef[rows_of(dom)]
    reduced_out[...] = part[rows_of(dom)]

    def add_coef(step, carry):
        coef_copy(doms - step).wait_recv()
        coef_out[...] += coef_in[step - 1]
        return carry

    lax.fori_loop(1, doms, add_coef, 0)

    def add_part(step, carry):
        pltpu.make_async_remote_copy(
            part.at[rows_of(0)], part_in.at[step - 1], part_send.at[0], part_recv.at[step - 1],
            at_dom(lax.rem(dom + 1, doms)), MESH,
        ).wait_recv()
        reduced_out[...] += part_in[step - 1]
        return carry

    lax.fori_loop(1, doms, add_part, 0)
    reduced_out[...] = reduced_out[...] * scaling

    for copy in gathers:
        copy.wait_send()

    @pl.when(dom < doms - 1)
    def _():
        up.wait_send()

    @pl.when(dom > 0)
    def _():
        down.wait_send()

    def end_coef(step, carry):
        coef_copy(step).wait_send()
        return carry

    lax.fori_loop(1, doms, end_coef, 0)

    def end_part(target, carry):
        @pl.when(target != dom)
        def _():
            part_copy(target).wait_send()

        return carry

    lax.fori_loop(0, doms, end_part, 0)


def solution(mesh):
    doms, modes = mesh.shape["dom"], mesh.shape["mode"]

    def shards(mode_basis, blocks, columns, samples, inverse):
        modes_here, nodes = mode_basis.shape[1:]
        halo = nodes // 4
        count = inverse.shape[0]
        mode_rows, coef_rows = modes * modes_here // doms, count // doms
        scaling = 1.0 / math.sqrt(3 * nodes * doms)
        vmem = pl.BlockSpec(memory_space=pltpu.VMEM)
        dma = pltpu.SemaphoreType.DMA
        return pl.pallas_call(
            functools.partial(kernel, doms, modes, halo, scaling),
            out_shape=(
                jax.ShapeDtypeStruct((mode_rows, modes_here), F32),
                jax.ShapeDtypeStruct((coef_rows, modes_here), F32),
            ),
            in_specs=[pl.BlockSpec(memory_space=pl.ANY), vmem, vmem, vmem, vmem],
            out_specs=(vmem, vmem),
            scratch_shapes=[
                pltpu.VMEM((3, modes_here, nodes + 2 * halo), BF16),
                pltpu.VMEM((modes - 1, 3, modes_here, nodes), BF16),
                pltpu.VMEM((3, modes_here, nodes), BF16),
                pltpu.VMEM((3, LANES + 2 * halo, 3 * LANES), BF16),
                pltpu.VMEM((blocks.shape[0], 9, 16, LANES), BF16),
                pltpu.VMEM((nodes, count), BF16),
                pltpu.VMEM((modes_here, count), F32),
                pltpu.VMEM((count, modes_here), F32),
                pltpu.VMEM((modes * modes_here, modes_here), F32),
                pltpu.VMEM((doms - 1, coef_rows, modes_here), F32),
                pltpu.VMEM((doms - 1, mode_rows, modes_here), F32),
                dma, dma((2,)), dma((2,)), dma((modes - 1, 3)), dma((modes - 1, 3)),
                dma((doms - 1,)), dma((doms - 1,)), dma((doms,)), dma((doms - 1,)),
            ],
            compiler_params=pltpu.CompilerParams(
                collective_id=0, has_side_effects=True, vmem_limit_bytes=48 * 1024 * 1024
            ),
        )(mode_basis, blocks, columns, samples.reshape(1, count), inverse)

    return jax.shard_map(
        shards,
        mesh=mesh,
        in_specs=(P(None, "mode", "dom"), P(None, None, None, "dom"), P(None, "dom"), P(), P()),
        out_specs=(P("dom", "mode"), P("dom", "mode")),
        check_vma=False,
    )
```

time: 536 us -> 60.5 us (0.11)
  the two profiles are of different devices: /device:TPU:0 before, /device:TPU:13 now
where the time goes in v1:
time: 60.5 us; the launch traced here: 60.2 us
  Pallas kernels  53.2 us (88%)
  local copies, waits for them, and re-layouts  6.42 us (11%)
  between operations  0.65 us (1%)
    pallas_call x1, Pallas kernels, shards(): pl.pallas_call(functools.partial(kernel, doms, modes, halo, scaling), out...  53.2 us
    unnamed x11, local copies, waits for them, and re-layouts  6.42 us

profile of v1, /device:TPU:13, one launch (start us, length us, event | category | flops | bytes accessed | tf_op | source)
XLA Modules:
  0.0 60.2 jit_solution(9225892223543509049)
XLA Ops:
  0.6 1.2 %copy.7.blocks = bf16[16,3,3,1024]{3,2,1,0:T(4,128)(2,1)S(1)} copy(bf16[16,3,3,1024]{3,0,2,1:T(8,128)(2,1)} %param.6) | data formatting | bytes 589824 | tf_op args[1]
  1.9 0.0 copy-start
  1.9 1.4 %copy-done = bf16[3,256,1024]{2,1,0:T(8,128)(2,1)S(1)} copy-done((bf16[3,256,1024]{2,1,0:T(8,128)(2,1)S(1)}, bf16[3,256,1024]{2,1,0:T(8,128)(2,1)}, u32[]{:S(2)}) %copy-start) | copy-done | bytes 1572888
  3.3 0.0 copy-start.1
  3.3 1.0 %copy-done.1 = bf16[512,512]{1,0:T(8,128)(2,1)S(1)} copy-done((bf16[512,512]{1,0:T(8,128)(2,1)S(1)}, bf16[512,512]{1,0:T(8,128)(2,1)}, u32[]{:S(2)}) %copy-start.1) | copy-done | bytes 524312
  4.3 0.0 copy-start.2
  4.3 0.8 %copy-done.2 = s32[16,1024]{1,0:T(8,128)S(1)} copy-done((s32[16,1024]{1,0:T(8,128)S(1)}, s32[16,1024]{1,0:T(8,128)}, u32[]{:S(2)}) %copy-start.2) | copy-done | bytes 65560
  5.1 0.0 copy-start.3
  5.1 0.7 %copy-done.3 = s32[512]{0:T(512)S(1)} copy-done((s32[512]{0:T(512)S(1)}, s32[512]{0:T(512)}, u32[]{:S(2)}) %copy-start.3) | copy-done | bytes 2072
  5.8 53.2 %shard_map.68 = (f32[32,256]{1,0:T(8,128)S(1)}, f32[32,256]{1,0:T(8,128)S(1)}) custom-call(bf16[3,256,1024]{2,1,0:T(8,128)(2,1)S(1)} %copy-done, bf16[16,3,3,1024]{3,2,1,0:T(4,128)(2,1)S(1)} %copy.7.blocks, s32[16,1024]{1,0:T(8,128)S(1)} %copy-done.2, s32[1,512]{1,0:T(1,128)S(1)} %bitcast.1, bf16[512,512]{1,0:T(8,128)(2,1)S(1)} %copy-done.1), custom_call_target="tpu_custom_call" | custom-call | tf_op jit(solution)/shard_map/pallas_call | solution.py:291
  59.0 0.6 %copy.10 = f32[32,256]{1,0:T(8,128)} copy(f32[32,256]{1,0:T(8,128)S(1)} %get-tuple-element.4) | data formatting | bytes 65536
  59.6 0.6 %copy.11 = f32[32,256]{1,0:T(8,128)} copy(f32[32,256]{1,0:T(8,128)S(1)} %get-tuple-element.5) | data formatting | bytes 65536
Async XLA Ops:
  1.9 1.4 %copy-start = (bf16[3,256,1024]{2,1,0:T(8,128)(2,1)S(1)}, bf16[3,256,1024]{2,1,0:T(8,128)(2,1)}, u32[]{:S(2)}) copy-start(bf16[3,256,1024]{2,1,0:T(8,128)(2,1)} %basis.1) | copy-start | bytes 4718596
  3.3 1.0 %copy-start.1 = (bf16[512,512]{1,0:T(8,128)(2,1)S(1)}, bf16[512,512]{1,0:T(8,128)(2,1)}, u32[]{:S(2)}) copy-start(bf16[512,512]{1,0:T(8,128)(2,1)} %inverse.1) | copy-start | bytes 1572868
  4.3 0.8 %copy-start.2 = (s32[16,1024]{1,0:T(8,128)S(1)}, s32[16,1024]{1,0:T(8,128)}, u32[]{:S(2)}) copy-start(s32[16,1024]{1,0:T(8,128)} %columns.1) | copy-start | bytes 196612
  5.1 0.7 %copy-start.3 = (s32[512]{0:T(512)S(1)}, s32[512]{0:T(512)}, u32[]{:S(2)}) copy-start(s32[512]{0:T(512)} %param.8) | copy-start | bytes 6148

commit v2 on v1

v2 whole, which is shorter than its diff:
```python
import functools
import math

import jax
import jax.numpy as jnp
from jax import lax
from jax.experimental import pallas as pl
from jax.experimental.pallas import tpu as pltpu
from jax.sharding import PartitionSpec as P

MESH = pl.DeviceIdType.MESH
LANES = 128
ROWS = 64
F32, BF16 = jnp.float32, jnp.bfloat16


def dot_nt(a, b):
    return lax.dot_general(a, b, (((1,), (1,)), ((), ())), preferred_element_type=F32)


def kernel(
    doms, modes, halo, scaling,
    basis, blocks_hbm, columns_hbm, samples_hbm, inverse_hbm,
    reduced_out, coef_out,
    blocks, columns, samples, inverse, ext, other, image, weights, spread, onehot, chosen, coef, part, coef_in, part_in, coef_twin, part_twin,
    local_sem, load_sem, halo_send, halo_recv, gather_send, gather_recv,
    coef_send, coef_recv, part_send, part_recv, twin_send, twin_recv,
):
    slots = columns.shape[0]
    modes_here, nodes = basis.shape[1], basis.shape[2]
    rows = reduced_out.shape[0]
    chunks = doms // modes // 2
    chunk = modes_here // chunks
    window = LANES + 2 * halo
    tiles = nodes // LANES
    dom, mode = lax.axis_index("dom"), lax.axis_index("mode")

    def at_dom(target):
        return (target, mode)

    barrier = pltpu.get_barrier_semaphore()

    def greet(step, carry):
        pl.semaphore_signal(barrier, inc=1, device_id=at_dom(lax.rem(dom + step, doms)), device_id_type=MESH)
        return carry

    lax.fori_loop(1, doms, greet, 0)
    for step in range(1, modes):
        pl.semaphore_signal(barrier, inc=1, device_id=(dom, lax.rem(mode + step, modes)), device_id_type=MESH)

    local = pltpu.make_async_copy(basis, ext.at[:, :, pl.ds(halo, nodes)], local_sem)
    loads = [
        pltpu.make_async_copy(columns_hbm, columns, load_sem.at[0]),
        pltpu.make_async_copy(blocks_hbm, blocks, load_sem.at[1]),
        pltpu.make_async_copy(samples_hbm, samples, load_sem.at[2]),
        pltpu.make_async_copy(inverse_hbm, inverse, load_sem.at[3]),
    ]
    for load in loads[:2]:
        load.start()
    local.start()
    for load in loads[2:]:
        load.start()
    pl.semaphore_wait(barrier, doms + modes - 2)

    up = pltpu.make_async_remote_copy(
        basis.at[:, :, pl.ds(nodes - halo, halo)], ext.at[:, :, pl.ds(0, halo)],
        halo_send.at[0], halo_recv.at[0], at_dom(lax.rem(dom + 1, doms)), MESH,
    )
    down = pltpu.make_async_remote_copy(
        basis.at[:, :, pl.ds(0, halo)], ext.at[:, :, pl.ds(halo + nodes, halo)],
        halo_send.at[1], halo_recv.at[1], at_dom(lax.rem(dom + doms - 1, doms)), MESH,
    )

    @pl.when(dom < doms - 1)
    def _():
        up.start()

    @pl.when(dom > 0)
    def _():
        down.start()

    gathers = []
    spans = [
        pl.ds(pl.multiple_of(lax.rem(dom // 2 + piece, chunks) * chunk, 16), chunk) for piece in range(chunks)
    ]
    for step in range(1, modes):
        for piece in range(chunks):
            copy = pltpu.make_async_remote_copy(
                basis.at[:, spans[piece]], other.at[step - 1, :, spans[piece]],
                gather_send.at[step - 1, piece], gather_recv.at[step - 1, piece],
                (dom, lax.rem(mode + step, modes)), MESH,
            )
            copy.start()
            gathers.append(copy)

    @pl.when(dom == 0)
    def _():
        ext[:, :, pl.ds(0, halo)] = jnp.zeros((3, modes_here, halo), BF16)

    @pl.when(dom == doms - 1)
    def _():
        ext[:, :, pl.ds(halo + nodes, halo)] = jnp.zeros((3, modes_here, halo), BF16)

    row_ids = (
        lax.broadcasted_iota(jnp.int32, (ROWS // 16, 16, LANES), 0) * 16
        + lax.broadcasted_iota(jnp.int32, (ROWS // 16, 16, LANES), 1)
    ).astype(F32).astype(BF16)
    lane_ids = lax.broadcasted_iota(jnp.int32, (slots, LANES), 1)
    slot_ids = lax.broadcasted_iota(jnp.int32, (slots, LANES), 0)
    unused = -8 * halo - slot_ids
    loads[0].wait()
    loads[1].wait()

    def tile_step(step, carry):
        tile = lax.rem(step + tiles // 4, tiles)
        start = pl.multiple_of(tile * LANES, LANES)
        here = pl.ds(start, LANES)

        offsets = columns[:, here]
        offsets = jnp.where(offsets == halo + 1, unused, offsets)
        values = [blocks[k // 3, k % 3, :, here].astype(F32) for k in range(9)]
        sums = list(values)
        repeated = offsets < -16 * halo
        for shift in range(1, slots):
            later = pltpu.roll(offsets, slots - shift, 0)
            same = (later == offsets) & (slot_ids < slots - shift)
            for k in range(9):
                sums[k] = sums[k] + jnp.where(same, pltpu.roll(values[k], slots - shift, 0), 0.0)
            earlier = pltpu.roll(offsets, shift, 0)
            repeated = repeated | ((earlier == offsets) & (slot_ids >= shift))
        offsets = jnp.where(repeated, unused, offsets)
        for j in range(slots):
            for k in range(9):
                spread[j, k] = jnp.broadcast_to(sums[k][j:j + 1], (16, LANES)).astype(BF16)
        places = (offsets + lane_ids + halo).astype(F32)

        def row_step(segment, inner):
            base = (segment * ROWS).astype(F32)
            sums = [jnp.zeros((ROWS // 16, 16, LANES), BF16) for _ in range(9)]
            for j in range(slots):
                place = jnp.broadcast_to(places[j:j + 1] - base, (16, LANES)).astype(BF16)
                hit = row_ids == place[None]
                for k in range(9):
                    sums[k] = jnp.where(hit, spread[j, k][None], sums[k])
            span = pl.ds(pl.multiple_of(segment * ROWS, ROWS), ROWS)
            for a in range(3):
                for b in range(3):
                    weights[b, span, a * LANES:(a + 1) * LANES] = sums[3 * a + b].reshape(ROWS, LANES)
            return inner

        lax.fori_loop(0, window // ROWS, row_step, 0)

        @pl.when(step == 0)
        def _():
            local.wait()

        @pl.when(step == tiles // 2)
        def _():
            @pl.when(dom > 0)
            def _():
                up.wait_recv()

            @pl.when(dom < doms - 1)
            def _():
                down.wait_recv()

        total = jnp.zeros((modes_here, 3 * LANES), F32)
        for b in range(3):
            total = total + jnp.dot(
                ext[b, :, pl.ds(start, window)], weights[b], preferred_element_type=F32
            )
        for a in range(3):
            image[a, :, here] = total[:, a * LANES:(a + 1) * LANES].astype(BF16)
        return carry

    lax.fori_loop(0, tiles, tile_step, 0)

    loads[2].wait()
    loads[3].wait()

    dofs = samples[...] - 3 * nodes * dom
    sample_count = dofs.shape[1]
    chosen[...] = jnp.zeros_like(chosen)
    node_ids = 3 * lax.broadcasted_iota(jnp.int32, (LANES, sample_count), 0)
    for c in range(3):
        def mark(tile, carry):
            found = node_ids == dofs - (3 * LANES * tile + c)
            onehot[pl.ds(pl.multiple_of(tile * LANES, LANES), LANES), :] = jnp.where(found, 1.0, 0.0).astype(BF16)
            return carry

        lax.fori_loop(0, tiles, mark, 0)
        chosen[...] += jnp.dot(image[c], onehot[...], preferred_element_type=F32)
    share = dot_nt(inverse[...], chosen[...].astype(BF16))
    for target in range(doms):
        coef[target % 2, pl.ds(target // 2 * rows, rows)] = share[target * rows:(target + 1) * rows]

    pairs = doms // 2
    pair, side = dom // 2, lax.rem(dom, 2)
    twin = dom + 1 - 2 * side

    def rows_of(target_pair):
        return pl.ds(pl.multiple_of(target_pair * rows, 8), rows)

    coef_swap = pltpu.make_async_remote_copy(
        coef.at[1 - side], coef_twin, twin_send.at[pairs], twin_recv.at[pairs], at_dom(twin), MESH,
    )
    coef_swap.start()

    def part_swap(target):
        return pltpu.make_async_remote_copy(
            part.at[1 - side, rows_of(target)], part_twin.at[rows_of(target)],
            twin_send.at[target], twin_recv.at[target], at_dom(twin), MESH,
        )

    def share_copy(source, landing, send, recv, step):
        target = lax.rem(pair + step, pairs)
        slot = pairs - step - 1
        return pltpu.make_async_remote_copy(
            source.at[side, rows_of(target)], landing.at[slot], send.at[step - 1], recv.at[slot],
            at_dom(2 * target + side), MESH,
        )

    def coef_copy(step):
        return share_copy(coef, coef_in, coef_send, coef_recv, step)

    def part_copy(step):
        return share_copy(part, part_in, part_send, part_recv, step)

    def begin(target, total):
        part[0, rows_of(target)] = total[:rows]
        part[1, rows_of(target)] = total[rows:]
        part_swap(target).start()

    def finish(target):
        swap = part_swap(target)
        swap.wait_recv()
        swap.wait_send()
        part[side, rows_of(target)] += part_twin[rows_of(target)]

        @pl.when(target != pair)
        def _():
            part_copy(lax.rem(target - pair + pairs, pairs)).start()

    total = jnp.zeros((modes_here, modes_here), F32)
    for c in range(3):
        total = total + dot_nt(ext[c, :, pl.ds(halo, nodes)], image[c])
    for place in range(chunks):
        begin(mode * chunks + place, total[place * chunk:(place + 1) * chunk])

    coef_swap.wait_recv()
    coef_swap.wait_send()
    coef[side] += coef_twin[...]

    def send_coef(step, carry):
        coef_copy(step).start()
        return carry

    lax.fori_loop(1, pairs, send_coef, 0)
    for place in range(chunks):
        finish(mode * chunks + place)

    pending = None
    for step in range(1, modes):
        block = lax.rem(mode + modes - step, modes)
        for piece in range(chunks):
            gathers[(step - 1) * chunks + piece].wait_recv()
            total = jnp.zeros((chunk, modes_here), F32)
            for c in range(3):
                total = total + dot_nt(other[step - 1, c, spans[piece]], image[c])
            target = block * chunks + lax.rem(pair + piece, chunks)
            begin(target, total)
            if pending is not None:
                finish(pending)
            pending = target
    if pending is not None:
        finish(pending)

    coef_out[...] = coef[side, rows_of(pair)]
    reduced_out[...] = part[side, rows_of(pair)]

    def add_coef(step, carry):
        coef_copy(pairs - step).wait_recv()
        coef_out[...] += coef_in[step - 1]
        return carry

    lax.fori_loop(1, pairs, add_coef, 0)

    def add_part(step, carry):
        part_copy(pairs - step).wait_recv()
        reduced_out[...] += part_in[step - 1]
        return carry

    lax.fori_loop(1, pairs, add_part, 0)
    reduced_out[...] = reduced_out[...] * scaling

    for copy in gathers:
        copy.wait_send()

    @pl.when(dom < doms - 1)
    def _():
        up.wait_send()

    @pl.when(dom > 0)
    def _():
        down.wait_send()

    def end_shares(step, carry):
        coef_copy(step).wait_send()
        part_copy(step).wait_send()
        return carry

    lax.fori_loop(1, pairs, end_shares, 0)


def solution(mesh):
    doms, modes = mesh.shape["dom"], mesh.shape["mode"]

    def shards(mode_basis, blocks, columns, samples, inverse):
        modes_here, nodes = mode_basis.shape[1:]
        halo = nodes // 4
        count = inverse.shape[0]
        mode_rows, coef_rows = modes * modes_here // doms, count // doms
        scaling = 1.0 / math.sqrt(3 * nodes * doms)
        vmem = pl.BlockSpec(memory_space=pltpu.VMEM)
        dma = pltpu.SemaphoreType.DMA
        return pl.pallas_call(
            functools.partial(kernel, doms, modes, halo, scaling),
            out_shape=(
                jax.ShapeDtypeStruct((mode_rows, modes_here), F32),
                jax.ShapeDtypeStruct((coef_rows, modes_here), F32),
            ),
            in_specs=[pl.BlockSpec(memory_space=pltpu.HBM)] * 5,
            out_specs=(vmem, vmem),
            scratch_shapes=[
                pltpu.VMEM((3, 3, blocks.shape[0], nodes), BF16),
                pltpu.VMEM(columns.shape, jnp.int32),
                pltpu.VMEM((1, count), jnp.int32),
                pltpu.VMEM(inverse.shape, BF16),
                pltpu.VMEM((3, modes_here, nodes + 2 * halo), BF16),
                pltpu.VMEM((modes - 1, 3, modes_here, nodes), BF16),
                pltpu.VMEM((3, modes_here, nodes), BF16),
                pltpu.VMEM((3, LANES + 2 * halo, 3 * LANES), BF16),
                pltpu.VMEM((blocks.shape[0], 9, 16, LANES), BF16),
                pltpu.VMEM((nodes, count), BF16),
                pltpu.VMEM((modes_here, count), F32),
                pltpu.VMEM((2, count // 2, modes_here), F32),
                pltpu.VMEM((2, modes * modes_here // 2, modes_here), F32),
                pltpu.VMEM((doms // 2 - 1, coef_rows, modes_here), F32),
                pltpu.VMEM((doms // 2 - 1, mode_rows, modes_here), F32),
                pltpu.VMEM((count // 2, modes_here), F32),
                pltpu.VMEM((modes * modes_here // 2, modes_here), F32),
                dma, dma((4,)), dma((2,)), dma((2,)), dma((modes - 1, doms // modes // 2)), dma((modes - 1, doms // modes // 2)),
                *[dma((doms // 2 - 1,))] * 4, *[dma((doms // 2 + 1,))] * 2,
            ],
            compiler_params=pltpu.CompilerParams(
                collective_id=0, has_side_effects=True, vmem_limit_bytes=62 * 1024 * 1024
            ),
        )(mode_basis, jnp.transpose(blocks, (1, 2, 0, 3)), columns, samples.reshape(1, count), inverse)

    return jax.shard_map(
        shards,
        mesh=mesh,
        in_specs=(P(None, "mode", "dom"), P(None, None, None, "dom"), P(None, "dom"), P(), P()),
        out_specs=(P("dom", "mode"), P("dom", "mode")),
        check_vma=False,
    )
```

time: 60.5 us -> 50.7 us (0.84)
  the two profiles are of different devices: /device:TPU:13 before, /device:TPU:0 now
where the time goes in v2:
time: 50.7 us; the launch traced here: 50.5 us
  Pallas kernels  47.1 us (93%)
  local copies, waits for them, and re-layouts  2.75 us (5%)
  between operations  0.64 us (1%)
    pallas_call x1, Pallas kernels, shards(): pl.pallas_call(functools.partial(kernel, doms, modes, halo, scaling), out...  47.1 us
    unnamed x2, local copies, waits for them, and re-layouts  2.75 us

profile of v2, /device:TPU:0, one launch (start us, length us, event | category | flops | bytes accessed | tf_op | source)
XLA Modules:
  0.0 50.5 jit_solution(4768719527975173189)
XLA Ops:
  0.6 47.1 %shard_map.68 = (f32[32,256]{1,0:T(8,128)}, f32[32,256]{1,0:T(8,128)}) custom-call(bf16[3,256,1024]{2,1,0:T(8,128)(2,1)} %basis.1, bf16[3,3,16,1024]{3,2,1,0:T(8,128)(2,1)} %bitcast.2, s32[16,1024]{1,0:T(8,128)} %columns_hbm.1, s32[1,512]{1,0:T(1,128)} %bitcast.3, bf16[512,512]{1,0:T(8,128)(2,1)} %inverse_hbm.1), custom_call_target="tpu_custom_call" | custom-call | tf_op jit(solution)/shard_map/pallas_call | solution.py:326
  47.7 1.4 %copy.9 = f32[32,256]{1,0:T(8,128)} copy(f32[32,256]{1,0:T(8,128)} %get-tuple-element.4) | data formatting | bytes 65536
  49.1 1.4 %copy.10 = f32[32,256]{1,0:T(8,128)} copy(f32[32,256]{1,0:T(8,128)} %get-tuple-element.5) | data formatting | bytes 65536
